TPU v7x, 256 devices: a whole 4x4x8 slice. The times are simulated.
256 devices in a mesh: pb: 16 (over y_hi, z), ka: 16 (over x, y_lo, core).
Axes of the slice: x: 4, y: 4 (y_hi: 2, y_lo: 2; y = y_hi * 2 + y_lo), z: 8, core: 2. Of those that a mesh axis runs over, the one named last changes fastest.
Arguments:
- tokens: bfloat16 [16, 2048, 768], P('ka', 'pb'), may hold values from -6 to 6
- pair: bfloat16 [2048, 2048, 128], P('pb', 'ka'), may hold values from -500 to 500
- token_chain_index: int32 [2048], replicated, may hold values from 0 to 7, never falling along the last dimension, each value on 1 to 1024 neighbouring positions
- key_mask: int32 [2048], replicated, may hold values 0 or 1
- norm_gain: float32 [768], replicated, may hold values from 0.25 to 1.75
- pair_gain: float32 [128], replicated, may hold values from 0.1 to 1.9
- pair_proj: float32 [128, 16], replicated, may hold values from -0.140625 to 0.140625
- chain_gain: float32 [16], replicated, may hold values from -2 to 260
- w_qkvg: bfloat16 [768, 3072], replicated, may hold values from -0.21875 to 0.21875
- w_out: bfloat16 [768, 768], replicated, may hold values from -1.75 to 1.75
Outputs:
- update: bfloat16 [16, 2048, 768], P('ka', 'pb')
Inputs may be any that keep to these rules, and one draw needn't show every extreme that they name: `token_chain_index`: chain ids never fall along the tokens.
All inputs are finite; a program needn't handle non-finite values.
Results may differ from a plain program's by a relative error of at most 0.02.
Values may be sent and summed in bfloat16 or wider, within the bound.
No kernel may reach another device: no remote copies, remote signals or barrier semaphores. Data moves between devices by JAX's collectives and lax.ppermute only.
A program may use at most 128 MiB of HBM per device.

v0:
```python
import jax
import jax.numpy as jnp
from jax import lax
from jax.sharding import PartitionSpec as P

epsilon = 1e-05


def norm_rows(values, gain):
    values = values.astype(jnp.float32)
    center = jnp.mean(values, axis=-1, keepdims=True)
    spread = jnp.mean(jnp.square(values - center), axis=-1, keepdims=True)
    return (values - center) * lax.rsqrt(spread + epsilon) * gain


def pair_bias(pair_rows, pair_gain, pair_proj, chain_query, chain_keys, chain_gain):
    zhat = norm_rows(pair_rows, pair_gain)
    head_bias = jnp.einsum("qkc,ch->hqk", zhat, pair_proj, precision=lax.Precision.HIGHEST)
    same = (chain_query[:, None] == chain_keys[None, :]).astype(jnp.float32)
    return head_bias + chain_gain[:, None, None] * same[None]


def apply_attention(query_vectors, keys, values, bias, key_mask, heads):
    q_count = query_vectors.shape[0]
    k_count = keys.shape[0]
    width = query_vectors.shape[1]
    hdim = width // heads
    query_heads = query_vectors.reshape(q_count, heads, hdim)
    key_heads = keys.reshape(k_count, heads, hdim)
    value_heads = values.reshape(k_count, heads, hdim)
    scores = jnp.einsum("qhd,khd->hqk", query_heads, key_heads, preferred_element_type=jnp.float32)
    scores = scores * hdim ** (-0.5) + bias
    scores = jnp.where(key_mask[None, None, :] > 0, scores, jnp.float32(-1000000000.0))
    top = jnp.max(scores, axis=-1, keepdims=True)
    expo = jnp.exp(scores - top)
    total = jnp.sum(expo, axis=-1)
    summed = jnp.einsum(
        "hqk,khd->qhd", expo.astype(jnp.bfloat16), value_heads, preferred_element_type=jnp.float32
    )
    return (summed / jnp.transpose(total)[:, :, None]).reshape(q_count, width)


def body(
    tokens,
    pair,
    token_chain_index,
    key_mask,
    norm_gain,
    pair_gain,
    pair_proj,
    chain_gain,
    w_qkvg,
    w_out,
):
    width = tokens.shape[2]
    q_count = tokens.shape[1]
    k_count = pair.shape[1]
    heads = chain_gain.shape[0]
    normalized_input = norm_rows(tokens, norm_gain).astype(jnp.bfloat16)
    query_weight = w_qkvg[:, :width]
    w_pairs = w_qkvg[:, width : 3 * width]
    gate_weight = w_qkvg[:, 3 * width :]
    query_vectors = jnp.einsum(
        "fop,pu->fou", normalized_input, query_weight, preferred_element_type=jnp.float32
    ).astype(jnp.bfloat16)
    gate_values = jnp.einsum(
        "fop,pu->fou", normalized_input, gate_weight, preferred_element_type=jnp.float32
    ).astype(jnp.bfloat16)
    row_start = lax.axis_index("pb") * q_count
    col_start = lax.axis_index("ka") * k_count
    chain_query = lax.dynamic_slice_in_dim(token_chain_index, row_start, q_count)
    chain_keys = lax.dynamic_slice_in_dim(token_chain_index, col_start, k_count)
    bias = pair_bias(pair, pair_gain, pair_proj, chain_query, chain_keys, chain_gain)
    key_values = jnp.einsum(
        "fop,pu->fou",
        lax.all_gather(normalized_input, "pb", axis=1, tiled=True),
        w_pairs,
        preferred_element_type=jnp.float32,
    ).astype(jnp.bfloat16)
    bias_all = lax.all_gather(bias, "ka", axis=2, tiled=True)

    def one_sample(items):
        query_one, pairs_one = items
        return apply_attention(
            query_one, pairs_one[:, :width], pairs_one[:, width:], bias_all, key_mask, heads
        )

    attended = lax.map(one_sample, (query_vectors, key_values))
    hidden = (jax.nn.sigmoid(gate_values.astype(jnp.float32)) * attended).astype(jnp.bfloat16)
    return jnp.einsum("sqd,de->sqe", hidden, w_out, preferred_element_type=jnp.float32).astype(
        jnp.bfloat16
    )


def solution(mesh):
    in_specs = (P("ka", "pb", None), P("pb", "ka", None), P(), P(), P(), P(), P(), P(), P(), P())
    out_specs = P("ka", "pb", None)
    return jax.shard_map(body, mesh=mesh, in_specs=in_specs, out_specs=out_specs, check_vma=False)
```

profile of v0, /device:TPU:1, one launch (start us, length us, event | category | flops | bytes accessed | tf_op | source)
XLA Modules:
  0.0 251.6 jit_solution(10574960976641568531)
XLA Ops:
  6.5 1.1 convert_reduce_fusion.1
  7.7 1.1 fusion.60
  8.8 1.8 fusion.62
  10.6 0.0 all-gather.3.cloned.1.call-update
  10.7 0.0 all-gather.5.cloned.1.call-start
  10.7 0.9 fusion.70
  11.7 0.1 compare_convert_fusion
  11.7 3.6 %convert_reduce_fusion = f32[128,128]{1,0:T(8,128)S(1)} fusion(bf16[128,128,128]{2,1,0:T(8,128)(2,1)} %param.11), kind=kLoop, calls=%fused_computation.5 | loop fusion | flops 4177920 | bytes 4259840 | tf_op jit(solution)/shard_map/reduce_sum | solution.py:11
  15.4 4.8 %fusion.4 = f32[128,128]{1,0:T(8,128)S(1)} fusion(bf16[128,128,128]{2,1,0:T(8,128)(2,1)S(1)} %copy-done.1, f32[128,128]{1,0:T(8,128)S(1)} %broadcast_multiply_fusion), kind=kLoop, calls=%fused_computation.8 | loop fusion | flops 8372224 | bytes 4325376 | tf_op jit(solution)/shard_map/reduce_sum | solution.py:12
  20.2 0.0 copy-start.2
  20.2 9.9 %fusion.6 = f32[128,128,16]{1,2,0:T(8,128)S(1)} fusion(bf16[128,128,128]{2,1,0:T(8,128)(2,1)S(1)} %copy-done.1, f32[128]{0:T(128)S(1)} %copy-done.6, f32[128,128]{1,0:T(8,128)S(1)} %add_rsqrt_fusion, f32[128,128]{1,0:T(8,128)S(1)} %broadcast_multiply_fusion, f32[128,16]{0,1:T(8,128)S(1)} %copy-done.5), kind=kOutput, calls=%fused_computation.10 | convolution fusion | flops 411041792 | bytes 5382656 | tf_op jit(solution)/shard_map/qkc,ch->hqk/dot_general | solution.py:18
  30.2 0.0 copy-start.3
  30.2 1.3 bitcast_add_fusion
  31.5 0.0 all-gather.5.cloned.1.call-update
  31.5 1.6 fusion.47
  33.2 0.2 copy.13
  33.3 71.1 %all-gather.3.cloned.1.call-done = bf16[1,2048,768]{2,1,0:T(8,128)(2,1)} async-done(((bf16[1,128,768]{2,1,0:T(8,128)(2,1)}), bf16[1,2048,768]{2,1,0:T(8,128)(2,1)}) %all-gather.3.cloned.1.call-update) | async-done | bytes 3145744 | tf_op jit(solution)/shard_map/all_gather | solution.py:76
  104.4 7.5 %convolution_convert_fusion = bf16[2048,1536]{0,1:T(8,128)(2,1)S(1)} fusion(bf16[1,2048,768]{2,1,0:T(8,128)(2,1)} %all-gather.3.cloned.1.call-done, bf16[768,3072]{1,0:T(8,128)(2,1)} %param.18), kind=kOutput, calls=%fused_computation.13 | convolution fusion | flops 4834983936 | bytes 11796480 | tf_op jit(solution)/shard_map/fop,pu->fou/dot_general | solution.py:74
  111.9 3.2 %fusion.69 = (bf16[2048,768]{0,1:T(8,128)(2,1)}, bf16[2048,768]{0,1:T(8,128)(2,1)}) fusion(bf16[2048,1536]{0,1:T(8,128)(2,1)S(1)} %convolution_convert_fusion), kind=kLoop, calls=%fused_computation.55 | loop fusion | bytes 12582912 | tf_op jit(solution)/shard_map/while/body/eval_jaxpr/slice | solution.py:85
  115.1 93.2 %all-gather.5.cloned.1.call-done = f32[16,128,2048]{2,1,0:T(8,128)} async-done(((f32[16,128,128]{2,1,0:T(8,128)}), f32[16,128,2048]{2,1,0:T(8,128)}) %all-gather.5.cloned.1.call-update) | async-done | bytes 16777232 | tf_op jit(solution)/shard_map/all_gather | solution.py:80
  208.3 15.5 %fusion.71 = (f32[16,128]{1,0:T(8,128)S(1)}, f32[16,128,2048]{2,1,0:T(8,128)}) fusion(f32[16,128,2048]{2,1,0:T(8,128)} %all-gather.5.cloned.1.call-done, bf16[128,16,48]{0,2,1:T(8,128)(2,1)S(1)} %bitcast.31, bf16[2048,16,48]{0,2,1:T(8,128)(2,1)} %bitcast.30, pred[2048]{0:T(1024)(128)(4,1)S(1)} %broadcast_compare_fusion), kind=kOutput, calls=%fused_computation.57 | convolution fusion | flops 419428352 | bytes 36907008 | tf_op jit(solution)/shard_map/while/body/eval_jaxpr/qhd,khd->hqk/dot_general | solution.py:31
  223.8 8.1 %fusion = f32[16,128]{1,0:T(8,128)S(1)} fusion(f32[16,128,2048]{2,1,0:T(8,128)} %get-tuple-element.28, f32[16,128]{1,0:T(8,128)S(1)} %get-tuple-element.26), kind=kLoop, calls=%fused_computation.2 | loop fusion | flops 8386560 | bytes 16793600 | tf_op jit(solution)/shard_map/while/body/eval_jaxpr/reduce_sum | solution.py:36
  231.9 9.8 %fusion.55 = f32[128,16,48]{0,2,1:T(8,128)S(1)} fusion(bf16[2048,16,48]{0,2,1:T(8,128)(2,1)} %bitcast.29, f32[16,128,2048]{2,1,0:T(8,128)} %get-tuple-element.28, f32[16,128]{1,0:T(8,128)S(1)} %get-tuple-element.26, f32[128,16]{0,1:T(8,128)S(1)} %bitcast.33), kind=kOutput, calls=%fused_computation.36 | convolution fusion | flops 411140096 | bytes 20332544 | tf_op jit(solution)/shard_map/while/body/eval_jaxpr/hqk,khd->qhd/dot_general | solution.py:37
  241.8 3.0 %fusion.52 = bf16[1,128,768]{2,1,0:T(8,128)(2,1)} fusion(bf16[768,768]{1,0:T(8,128)(2,1)S(1)} %copy-done, f32[128,768]{0,1:T(8,128)S(1)} %bitcast.32, bf16[768,3072]{1,0:T(8,128)(2,1)} %param.18, bf16[1,128,768]{2,1,0:T(8,128)(2,1)S(1)} %copy-done.2), kind=kOutput, calls=%fused_computation.34 | convolution fusion | flops 302776320 | bytes 3145728 | tf_op jit(solution)/shard_map/sqd,de->sqe/dot_general | solution.py:90
  (18 shorter events, 0.1 us)
Async XLA Ops:
  6.5 235.3 %copy-start = (bf16[768,768]{1,0:T(8,128)(2,1)S(1)}, bf16[768,768]{1,0:T(8,128)(2,1)}, u32[]{:S(2)}) copy-start(bf16[768,768]{1,0:T(8,128)(2,1)} %param.19) | copy-start | bytes 3538948
  6.5 97.9 %all-gather.3.cloned.1.call-start = ((), (), s32[]{:S(2)}) async-start(), calls=%async_computation | async-start | bytes 3342336 | tf_op jit(solution)/shard_map/all_gather | solution.py:76
  8.8 11.4 %copy-start.5 = (f32[128,16]{0,1:T(8,128)S(1)}, f32[128,16]{0,1:T(8,128)}, u32[]{:S(2)}) copy-start(f32[128,16]{0,1:T(8,128)} %param.16) | copy-start | bytes 24580
  8.8 11.4 %copy-start.6 = (f32[128]{0:T(128)S(1)}, f32[128]{0:T(128)}, u32[]{:S(2)}) copy-start(f32[128]{0:T(128)} %param.15) | copy-start | bytes 1540
  10.7 197.7 %all-gather.5.cloned.1.call-start = ((), (), s32[]{:S(2)}) async-start(), calls=%async_computation.1 | async-start | bytes 17825792 | tf_op jit(solution)/shard_map/all_gather | solution.py:80
  10.7 4.7 %copy-start.1 = (bf16[128,128,128]{2,1,0:T(8,128)(2,1)S(1)}, bf16[128,128,128]{2,1,0:T(8,128)(2,1)}, u32[]{:S(2)}) copy-start(bf16[128,128,128]{2,1,0:T(8,128)(2,1)} %param.11) | copy-start | bytes 12582916
  20.2 10.0 %copy-start.4 = (f32[16]{0:T(128)S(1)}, f32[16]{0:T(128)}, u32[]{:S(2)}) copy-start(f32[16]{0:T(128)} %param.17) | copy-start | bytes 196
  20.2 11.3 %copy-start.2 = (bf16[1,128,768]{2,1,0:T(8,128)(2,1)S(1)}, bf16[1,128,768]{2,1,0:T(8,128)(2,1)}, u32[]{:S(2)}) copy-start(bf16[1,128,768]{2,1,0:T(8,128)(2,1)} %fusion.62) | copy-start | bytes 589828
  30.2 3.2 %copy-start.3 = (s32[2048]{0:T(1024)S(1)}, s32[2048]{0:T(1024)}, u32[]{:S(2)}) copy-start(s32[2048]{0:T(1024)} %param.13) | copy-start | bytes 24580
Sparse Core Ops, SparseCore 0:
  10.8 93.5 all-gather.2
  106.2 102.1 all-gather.4
where the time goes:
time: 252 us
  waiting for transfers between devices  164 us (65%)
  matrix products  47.3 us (19%)
  other arithmetic  22 us (9%)
  between operations  13.6 us (5%)
  local copies, waits for them, and re-layouts  4.3 us (2%)
    all_gather x1, waiting for transfers between devices, body(): bias_all = lax.all_gather(bias, 'ka', axis=2, tiled=True)  93.2 us
    all_gather x1, waiting for transfers between devices, body(): lax.all_gather(normalized_input, 'pb', axis=1, tiled=True)  71.1 us
    dot_general x1, matrix products, apply_attention(): jnp.einsum('qhd,khd->hqk', query_heads, key_heads, preferred_element_type...  15.5 us
    dot_general x1, matrix products, pair_bias(): jnp.einsum('qkc,ch->hqk', zhat, pair_proj, precision=lax.Precision.HIGHEST)  9.91 us
    dot_general x1, matrix products, apply_attention(): jnp.einsum('hqk,khd->qhd', expo.astype(jnp.bfloat16), value_heads, prefer...  9.84 us
    reduce_sum x1, other arithmetic, apply_attention(): total = jnp.sum(expo, axis=-1)  8.14 us
    dot_general x1, matrix products, body(): jnp.einsum('fop,pu->fou', lax.all_gather(normalized_input, 'pb', axis=1,...  7.49 us
    reduce_sum x2, other arithmetic, norm_rows(): spread = jnp.mean(jnp.square(values - center), axis=-1, keepdims=True)  5.9 us
  transfers between devices with their start and end apart: 2, of which 2 were waited for; matrix products, arithmetic and copies ran while one was open for 13% of the time, Pallas kernels for 0%

commit v1 on v0

--- a/solution.py
+++ b/solution.py
@@ -77,7 +77,9 @@
         w_pairs,
         preferred_element_type=jnp.float32,
     ).astype(jnp.bfloat16)
-    bias_all = lax.all_gather(bias, "ka", axis=2, tiled=True)
+    bias_all = jnp.concatenate(
+        lax.all_to_all(jnp.stack(lax.axis_size("ka") * [bias], 0), "ka", 0, 0), 2
+    )
 
     def one_sample(items):
         query_one, pairs_one = items

time: 252 us -> 356 us (1.41)
  waiting for transfers between devices: 164 us -> 257 us
  starting transfers between devices: 0.04 us -> 8.47 us
  local copies, waits for them, and re-layouts: 4.3 us -> 12.6 us
  other arithmetic: 22 us -> 17.7 us
    all_gather x1, waiting for transfers between devices: 71.1 us -> 185 us  [body(): lax.all_gather(normalized_input, 'pb', axis=1, tiled=True)]
    all_gather x1 -> x0, waiting for transfers between devices: 93.2 us -> none  [body(): bias_all = lax.all_gather(bias, 'ka', axis=2, tiled=True)]
    all_to_all x0 -> x1, waiting for transfers between devices: none -> 72.4 us  [body(): lax.all_to_all(jnp.stack(lax.axis_size('ka') * [bias], 0), 'ka', 0, 0)]
    all_to_all x0 -> x1, starting transfers between devices: none -> 8.25 us  [body(): lax.all_to_all(jnp.stack(lax.axis_size('ka') * [bias], 0), 'ka', 0, 0)]
    another operation x0 -> x1, local copies, waits for them, and re-layouts: none -> 7.83 us  [body(): jnp.stack(lax.axis_size('ka') * [bias], 0)]
  transfers between devices with their start and end apart: 2 -> 2, of which waited for: 2 -> 2; matrix products, arithmetic and copies ran while one was open for 13% -> 4% of each run, Pallas kernels for 0% -> 0%
where the time goes in v1:
time: 356 us; the launch traced here: 355 us
  waiting for transfers between devices  257 us (72%)
  matrix products  46 us (13%)
  other arithmetic  17.7 us (5%)
  between operations  13.6 us (4%)
  local copies, waits for them, and re-layouts  12.6 us (4%)
  starting transfers between devices  8.47 us (2%)
    all_gather x1, waiting for transfers between devices, body(): lax.all_gather(normalized_input, 'pb', axis=1, tiled=True)  185 us
    all_to_all x1, waiting for transfers between devices, body(): lax.all_to_all(jnp.stack(lax.axis_size('ka') * [bias], 0), 'ka', 0, 0)  72.4 us
    dot_general x1, matrix products, pair_bias(): jnp.einsum('qkc,ch->hqk', zhat, pair_proj, precision=lax.Precision.HIGHEST)  12.3 us
    dot_general x1, matrix products, apply_attention(): jnp.einsum('qhd,khd->hqk', query_heads, key_heads, preferred_element_type...  12 us
    dot_general x1, matrix products, apply_attention(): jnp.einsum('hqk,khd->qhd', expo.astype(jnp.bfloat16), value_heads, prefer...  9.87 us
    all_to_all x1, starting transfers between devices, body(): lax.all_to_all(jnp.stack(lax.axis_size('ka') * [bias], 0), 'ka', 0, 0)  8.25 us
    reduce_sum x1, other arithmetic, apply_attention(): total = jnp.sum(expo, axis=-1)  8.14 us
    another operation x1, local copies, waits for them, and re-layouts, body(): jnp.stack(lax.axis_size('ka') * [bias], 0)  7.83 us
  transfers between devices with their start and end apart: 2, of which 2 were waited for; matrix products, arithmetic and copies ran while one was open for 4% of the time, Pallas kernels for 0%

profile of v1, /device:TPU:1, one launch (start us, length us, event | category | flops | bytes accessed | tf_op | source)
XLA Modules:
  0.0 355.5 jit_solution(1330198322428591047)
XLA Ops:
  6.6 3.5 convert_reduce_fusion
  10.1 4.8 %fusion.5 = f32[128,128]{1,0:T(8,128)S(1)} fusion(bf16[128,128,128]{2,1,0:T(8,128)(2,1)S(1)} %copy-done.1, f32[128,128]{1,0:T(8,128)S(1)} %broadcast_multiply_fusion), kind=kLoop, calls=%fused_computation.9 | loop fusion | flops 8372224 | bytes 4325376 | tf_op jit(solution)/shard_map/reduce_sum | solution.py:12
  14.9 0.8 fusion.77
  15.7 0.1 compare_convert_fusion
  15.9 12.3 %fusion.20 = f32[16,128,128]{2,0,1:T(8,128)S(1)} fusion(bf16[128,128,128]{2,1,0:T(8,128)(2,1)} %param.11, f32[128]{0:T(128)S(1)} %copy-done.7, f32[128,128]{1,0:T(8,128)S(1)} %add_rsqrt_fusion, f32[128,128]{1,0:T(8,128)S(1)} %broadcast_multiply_fusion, f32[128,128]{1,0:T(8,128)S(1)} %compare_convert_fusion, f32[16]{0:T(128)S(1)} %copy-done.8, ...), kind=kOutput, calls=%fused_computation.21 | convolution fusion | flops 411566080 | bytes 5448256 | tf_op jit(solution)/shard_map/qkc,ch->hqk/dot_general | solution.py:18
  28.2 0.3 copy.20
  28.5 7.8 %stack.2 = f32[16,16,128,128]{3,2,1,0:T(8,128)} broadcast(f32[16,128,128]{2,1,0:T(8,128)S(1)} %copy.20), dimensions={1,2,3} | broadcast | bytes 17825792 | tf_op jit(solution)/shard_map/stack | solution.py:81
  36.4 8.3 %all-to-all-start = ((f32[16,16,128,128]{3,2,1,0:T(8,128)}), f32[16,16,128,128]{3,2,1,0:T(8,128)}, u32[]{:S(2)}, u32[]{:S(2)}) async-start(f32[16,16,128,128]{3,2,1,0:T(8,128)} %stack.2), calls=%async_computation | async-start | bytes 33554432 | tf_op jit(solution)/shard_map/all_to_all | solution.py:81
  44.6 0.2 all-gather.2.cloned.1.call-start
  44.9 0.1 convert_reduce_fusion.1
  45.0 0.2 fusion.67
  45.2 0.8 fusion.69
  46.1 0.0 all-gather.2.cloned.1.call-update
  46.1 1.7 fusion.54
  47.8 0.2 copy.19
  48.0 184.7 %all-gather.2.cloned.1.call-done = bf16[1,2048,768]{2,1,0:T(8,128)(2,1)} async-done(((bf16[1,128,768]{2,1,0:T(8,128)(2,1)}), bf16[1,2048,768]{2,1,0:T(8,128)(2,1)}) %all-gather.2.cloned.1.call-update) | async-done | bytes 3145744 | tf_op jit(solution)/shard_map/all_gather | solution.py:76
  232.7 7.5 %convolution_convert_fusion = bf16[2048,1536]{0,1:T(8,128)(2,1)S(1)} fusion(bf16[1,2048,768]{2,1,0:T(8,128)(2,1)} %all-gather.2.cloned.1.call-done, bf16[768,3072]{1,0:T(8,128)(2,1)} %param.18), kind=kOutput, calls=%fused_computation.14 | convolution fusion | flops 4834983936 | bytes 11796480 | tf_op jit(solution)/shard_map/fop,pu->fou/dot_general | solution.py:74
  240.2 3.2 fusion.76
  243.4 72.4 %all-to-all-done = f32[16,16,128,128]{3,2,1,0:T(8,128)} async-done(((f32[16,16,128,128]{3,2,1,0:T(8,128)}), f32[16,16,128,128]{3,2,1,0:T(8,128)}, u32[]{:S(2)}, u32[]{:S(2)}) %all-to-all-start) | async-done | bytes 16777248 | tf_op jit(solution)/shard_map/all_to_all | solution.py:81
  315.8 12.0 %fusion.78 = (f32[16,128]{1,0:T(8,128)S(1)}, f32[16,128,2048]{2,1,0:T(8,128)}) fusion(bf16[128,16,48]{0,2,1:T(8,128)(2,1)S(1)} %bitcast.42, bf16[2048,16,48]{0,2,1:T(8,128)(2,1)} %bitcast.40, pred[2048]{0:T(1024)(128)(4,1)S(1)} %broadcast_compare_fusion, f32[16,16,128,128]{3,2,1,0:T(8,128)} %all-to-all-done), kind=kOutput, calls=%fused_computation.59 | convolution fusion | flops 419428352 | bytes 36907008 | tf_op jit(solution)/shard_map/while/body/eval_jaxpr/qhd,khd->hqk/dot_general | solution.py:31
  327.8 8.1 %fusion.1 = f32[16,128]{1,0:T(8,128)S(1)} fusion(f32[16,128,2048]{2,1,0:T(8,128)} %get-tuple-element.28, f32[16,128]{1,0:T(8,128)S(1)} %get-tuple-element.26), kind=kLoop, calls=%fused_computation.3 | loop fusion | flops 8386560 | bytes 16793600 | tf_op jit(solution)/shard_map/while/body/eval_jaxpr/reduce_sum | solution.py:36
  336.0 9.9 %fusion.62 = f32[128,16,48]{0,2,1:T(8,128)S(1)} fusion(bf16[2048,16,48]{0,2,1:T(8,128)(2,1)} %bitcast.39, f32[16,128,2048]{2,1,0:T(8,128)} %get-tuple-element.28, f32[16,128]{1,0:T(8,128)S(1)} %get-tuple-element.26, f32[128,16]{0,1:T(8,128)S(1)} %bitcast.43), kind=kOutput, calls=%fused_computation.38 | convolution fusion | flops 411140096 | bytes 20332544 | tf_op jit(solution)/shard_map/while/body/eval_jaxpr/hqk,khd->qhd/dot_general | solution.py:37
  345.8 0.2 copy.22
  346.0 2.6 fusion.59
  (23 shorter events, 0.1 us)
Async XLA Ops:
  6.5 339.5 %copy-start = (bf16[768,768]{1,0:T(8,128)(2,1)S(1)}, bf16[768,768]{1,0:T(8,128)(2,1)}, u32[]{:S(2)}) copy-start(bf16[768,768]{1,0:T(8,128)(2,1)} %param.19) | copy-start | bytes 3538948
  6.5 9.3 %copy-start.8 = (f32[16]{0:T(128)S(1)}, f32[16]{0:T(128)}, u32[]{:S(2)}) copy-start(f32[16]{0:T(128)} %param.17) | copy-start | bytes 196
  6.5 9.3 %copy-start.6 = (f32[128,16]{0,1:T(8,128)S(1)}, f32[128,16]{0,1:T(8,128)}, u32[]{:S(2)}) copy-start(f32[128,16]{0,1:T(8,128)} %param.16) | copy-start | bytes 24580
  6.5 9.3 %copy-start.7 = (f32[128]{0:T(128)S(1)}, f32[128]{0:T(128)}, u32[]{:S(2)}) copy-start(f32[128]{0:T(128)} %param.15) | copy-start | bytes 1540
  6.5 3.5 copy-start.1
  36.4 8.5 %copy-start.2 = (bf16[1,128,768]{2,1,0:T(8,128)(2,1)S(1)}, bf16[1,128,768]{2,1,0:T(8,128)(2,1)}, u32[]{:S(2)}) copy-start(bf16[1,128,768]{2,1,0:T(8,128)(2,1)} %param.10) | copy-start | bytes 589828
  36.4 8.8 %copy-start.5 = (f32[768]{0:T(1024)S(1)}, f32[768]{0:T(1024)}, u32[]{:S(2)}) copy-start(f32[768]{0:T(1024)} %param.14) | copy-start | bytes 9220
  36.4 11.6 %copy-start.4 = (s32[2048]{0:T(1024)S(1)}, s32[2048]{0:T(1024)}, u32[]{:S(2)}) copy-start(s32[2048]{0:T(1024)} %param.13) | copy-start | bytes 24580
  36.4 279.4 %all-to-all-start = ((f32[16,16,128,128]{3,2,1,0:T(8,128)}), f32[16,16,128,128]{3,2,1,0:T(8,128)}, u32[]{:S(2)}, u32[]{:S(2)}) async-start(f32[16,16,128,128]{3,2,1,0:T(8,128)} %stack.2), calls=%async_computation | async-start | bytes 33554432 | tf_op jit(solution)/shard_map/all_to_all | solution.py:81
  44.6 188.1 %all-gather.2.cloned.1.call-start = ((), (), s32[]{:S(2)}) async-start(), calls=%async_computation.1 | async-start | bytes 3342336 | tf_op jit(solution)/shard_map/all_gather | solution.py:76
  336.0 10.1 %copy-start.3 = (bf16[1,128,768]{2,1,0:T(8,128)(2,1)S(1)}, bf16[1,128,768]{2,1,0:T(8,128)(2,1)}, u32[]{:S(2)}) copy-start(bf16[1,128,768]{2,1,0:T(8,128)(2,1)} %fusion.69) | copy-start | bytes 589828
Sparse Core Ops, SparseCore 0:
  48.1 184.6 all-gather.1
